TPU v7x, 32 devices: a whole 2x2x4 slice. The times are simulated.
32 devices in a mesh: groups: 2 (over y), ep: 4 (over z), tp: 4 (over x, core).
Axes of the slice: x: 2, y: 2, z: 4, core: 2. Of those that a mesh axis runs over, the one named last changes fastest.
Arguments:
- tokens: bfloat16 [384, 2048], P(('groups', 'ep'), 'tp'), parts along dimension 0, may hold values from -6 to 6
- norm_gain: float32 [2048], replicated, may hold values from 0.1 to 1.9
- route_ids: int32 [384, 8], P(('groups', 'ep')), parts along dimension 0, may hold values from 0 to 63, all different within a row; in each aligned block of 48 rows (0 to 47, 48 to 95, ...) at most 15 rows name the same one
- route_scores: float32 [384, 8], P(('groups', 'ep')), parts along dimension 0, may hold values from 0.05 to 1
- gate_weight: bfloat16 [128, 1024, 2048], P(('groups', 'ep'), 'tp'), parts along dimension 0, may hold values from -0.125 to 0.125
- up_weight: bfloat16 [128, 1024, 2048], P(('groups', 'ep'), 'tp'), parts along dimension 0, may hold values from -0.125 to 0.125
- down_weight: bfloat16 [128, 2048, 1024], P(('groups', 'ep'), None, 'tp'), parts along dimension 0, may hold values from -0.1875 to 0.1875
- delta_codes: bfloat16 [8, 4, 256, 128], P(('groups', 'ep'), 'tp'), parts along dimension 0, may hold values from -4 to 4
- delta_exps: int32 [8, 4, 256], P(('groups', 'ep'), 'tp'), parts along dimension 0, may hold values from -7 to -4
- delta_owner: int32 [8, 4, 256, 1], P(('groups', 'ep'), 'tp'), parts along dimension 0, may hold values from 0 to 3; in each aligned block of 256 rows (0 to 255, 256 to 511, ..., all dimensions but the last counted through in order) at most 160 rows name the same one
- delta_places: int32 [8, 4, 256], P(('groups', 'ep'), 'tp'), parts along dimension 0, may hold values from 0 to 49151
Outputs:
- mixed: bfloat16 [384, 2048], P(('groups', 'ep'), 'tp'), parts along dimension 0
There are 2 independent parts, one for each index of `groups`. A program takes and returns all parts, laid end to end along the dimension named above; an argument that names none is the same for every part. Nothing has to cross between parts.
Inputs may be any that keep to these rules, and one draw needn't show every extreme that they name: `route_ids`: each row names 8 different experts. In the 48 rows of one device (aligned blocks of 48 rows) no expert is named by more than 15 rows. `delta_owner`: in the 256 blocks of one learner shard (aligned blocks of 256 rows) no owner is named more than 160 times.
All inputs are finite; a program needn't handle non-finite values.
Results may differ from a plain program's by a relative error of at most 0.012.
Values may be sent and summed in bfloat16 or wider, within the bound.
A program may use at most 320 MiB of HBM per device.

v0:
```python
import jax
import jax.numpy as jnp
from jax import lax
from jax.sharding import PartitionSpec as P

EXPERTS = 64
TOP = 8
CAP = 15


EPS = 1e-06


def row_norm(values, gain, width):
    floats = values.astype(jnp.float32)
    scaling = lax.rsqrt(jnp.sum(floats * floats, axis=-1, keepdims=True) / width + EPS)
    return (floats * scaling * gain).astype(jnp.bfloat16)


def per_device(
    tokens,
    norm_gain,
    route_ids,
    route_scores,
    gate_weight,
    up_weight,
    down_weight,
    delta_codes,
    delta_exps,
    delta_owner,
    delta_places,
):
    ep_count = lax.axis_size("ep")
    ep_rank = lax.axis_index("ep")
    exp_dev, ff_local, width = gate_weight.shape
    block = delta_codes.shape[3]
    block_count = delta_codes.shape[2]
    per_row = width // block
    per_down = ff_local // block
    ff_rows = ff_local // ep_count
    d_rows = width // ep_count
    span = ff_rows * per_row
    places = 2 * span + d_rows * per_down
    bucket = block_count * 5 // (2 * ep_count)
    gate_blocks = exp_dev * ff_local * per_row
    table_rows = 3 * gate_blocks
    delta_values = (
        delta_codes[0, 0].astype(jnp.float32)
        * jnp.exp2(delta_exps[0, 0].astype(jnp.float32))[:, None]
    ).astype(jnp.bfloat16)
    placing = delta_places[0, 0]
    local_expert = placing // places
    spot = placing % places
    remain = spot % span
    matrix_pick = jnp.minimum(spot // span, 1)
    gate_slot = (
        matrix_pick * gate_blocks
        + (local_expert * ff_local + ep_rank * ff_rows + remain // per_row) * per_row
        + remain % per_row
    )
    down_spot = jnp.maximum(spot - 2 * span, 0)
    down_slot = (
        2 * gate_blocks
        + (local_expert * width + ep_rank * d_rows + down_spot // per_down) * per_down
        + down_spot % per_down
    )
    target = jnp.where(spot < 2 * span, gate_slot, down_slot)
    owners = delta_owner[0, 0, :, 0]
    owner_hits = (owners[:, None] == jnp.arange(ep_count, dtype=jnp.int32)[None, :]).astype(
        jnp.int32
    )
    owner_before = jnp.cumsum(owner_hits, axis=0) - owner_hits
    position = owners * bucket + jnp.sum(owner_before * owner_hits, axis=1)
    send_match = position[None, :] == jnp.arange(ep_count * bucket, dtype=jnp.int32)[:, None]
    send_values = jnp.dot(
        send_match.astype(jnp.bfloat16), delta_values, preferred_element_type=jnp.float32
    ).astype(jnp.bfloat16)
    target_code = jnp.dot(
        send_match.astype(jnp.float32),
        (target + 1).astype(jnp.float32),
        precision=lax.Precision.HIGHEST,
    ).astype(jnp.int32)
    send_target = jnp.where(target_code > 0, target_code - 1, table_rows)
    got_values, got_target = (
        lax.all_to_all(
            send_values.reshape(ep_count, bucket, block),
            "ep",
            split_axis=0,
            concat_axis=0,
            tiled=True,
        ),
        lax.all_to_all(
            send_target.reshape(ep_count, bucket), "ep", split_axis=0, concat_axis=0, tiled=True
        ),
    )
    got_flat = got_target.reshape(-1)
    got_rows = got_values.reshape(-1, block)
    same_target = (got_flat[:, None] == got_flat[None, :]).astype(jnp.bfloat16)
    combined = jnp.dot(same_target, got_rows, preferred_element_type=jnp.float32)

    def updated(weight, base):
        flat_weight = weight.reshape(-1, block)
        offset_ids = got_flat - base
        usable = jnp.logical_and(offset_ids >= 0, offset_ids < gate_blocks)
        row_index = jnp.where(usable, offset_ids, gate_blocks).astype(jnp.int32)
        fetched = jnp.take(flat_weight, jnp.minimum(row_index, gate_blocks - 1), axis=0).astype(
            jnp.float32
        )
        new_rows = (fetched + combined).astype(jnp.bfloat16)
        return flat_weight.at[row_index].set(new_rows, mode="drop").reshape(weight.shape)

    new_gate = updated(gate_weight, 0)
    new_up = updated(up_weight, gate_blocks)
    new_down = updated(down_weight, 2 * gate_blocks)
    token_rows, slice_width = tokens.shape
    picks = route_ids.reshape(-1)
    expert_hits = (picks[:, None] == jnp.arange(EXPERTS, dtype=jnp.int32)[None, :]).astype(
        jnp.int32
    )
    expert_before = jnp.cumsum(expert_hits, axis=0) - expert_hits
    slot = picks * CAP + jnp.sum(expert_before * expert_hits, axis=1)
    slot_match = (slot[None, :] == jnp.arange(EXPERTS * CAP, dtype=jnp.int32)[:, None]).reshape(
        EXPERTS * CAP, token_rows, TOP
    )
    full_rows = lax.all_gather(tokens, "tp", axis=1, tiled=True)
    outgoing = row_norm(full_rows, norm_gain, width)
    feature_count = outgoing.shape[1]
    slot_rows = jnp.any(slot_match, axis=2).astype(jnp.bfloat16)
    sending = jnp.dot(slot_rows, outgoing, preferred_element_type=jnp.float32).astype(jnp.bfloat16)
    sending = sending.reshape(ep_count, exp_dev, CAP, feature_count)
    normed = lax.all_to_all(sending, "ep", split_axis=0, concat_axis=0, tiled=True)
    gate = jnp.einsum("secd,efd->secf", normed, new_gate, preferred_element_type=jnp.float32)
    up = jnp.einsum("secd,efd->secf", normed, new_up, preferred_element_type=jnp.float32)
    gate, up = (gate, up)
    hidden = (jax.nn.silu(gate) * up).astype(jnp.bfloat16)
    partial_value = jnp.einsum(
        "secf,edf->secd", hidden, new_down, preferred_element_type=jnp.float32
    ).astype(jnp.bfloat16)
    results = lax.all_to_all(partial_value, "ep", split_axis=0, concat_axis=0, tiled=True)
    result_width = results.shape[3]
    flat_results = results.reshape(EXPERTS * CAP, result_width).astype(jnp.float32)
    shares = route_scores / jnp.sum(route_scores, axis=1, keepdims=True)
    slot_shares = jnp.sum(jnp.where(slot_match, shares[None, :, :], 0.0), axis=2)
    weighted = jnp.einsum("st,sd->td", slot_shares, flat_results, precision=lax.Precision.HIGHEST)
    return lax.psum_scatter(weighted.astype(jnp.bfloat16), "tp", scatter_dimension=1, tiled=True)


def solution(mesh):
    placed = (
        P(("groups", "ep"), "tp"),
        P(),
        P(("groups", "ep"), None),
        P(("groups", "ep"), None),
        P(("groups", "ep"), "tp", None),
        P(("groups", "ep"), "tp", None),
        P(("groups", "ep"), None, "tp"),
        P(("groups", "ep"), "tp", None, None),
        P(("groups", "ep"), "tp", None),
        P(("groups", "ep"), "tp", None, None),
        P(("groups", "ep"), "tp", None),
    )
    return jax.shard_map(
        per_device, mesh=mesh, in_specs=placed, out_specs=P(("groups", "ep"), "tp"), check_vma=False
    )
```

profile of v0, /device:TPU:0, one launch (start us, length us, event | category | flops | bytes accessed | tf_op | source)
XLA Modules:
  0.0 542.9 jit_solution(11301416206348084464)
XLA Ops:
  12.7 6.3 %all-to-all-start = ((s32[4,1,160]{2,1,0:T(1,128)}), s32[4,1,160]{2,1,0:T(1,128)S(1)}, u32[]{:S(2)}, u32[]{:S(2)}) async-start(s32[4,1,160]{2,1,0:T(1,128)} %all_to_all.15), calls=%async_computation | async-start | bytes 8192 | tf_op jit(solution)/shard_map/all_to_all | solution.py:92
  22.9 5.8 %all_gather.3 = bf16[48,2048]{1,0:T(8,128)(2,1)S(1)} all-gather(bf16[48,512]{1,0:T(8,128)(2,1)} %param.13), channel_id=1, replica_groups=mesh['groups'=2,'ep'=4,'tp'=4] {'tp'}, dimensions={1}, use_global_device_ids=true | all-gather | bytes 245760 | tf_op jit(solution)/shard_map/all_gather | solution.py:125
  31.3 5.1 all-to-all-start.1
  40.2 5.1 reshape.255
  45.3 6.4 %copy.61 = bf16[4,16,15,2048]{3,1,2,0:T(8,128)(2,1)} copy(bf16[4,16,15,2048]{3,2,1,0:T(8,128)(2,1)} %reshape.255) | data formatting | bytes 7864320 | tf_op jit(solution)/shard_map/reshape | solution.py:130
  51.7 5.3 all-to-all-start.2
  57.1 25.6 %reshape.253 = bf16[65536,128]{1,0:T(8,128)(2,1)} reshape(bf16[16,256,2048]{2,1,0:T(8,128)(2,1)} %param.17) | data formatting | bytes 33554432 | tf_op jit(solution)/shard_map/reshape | solution.py:102
  82.6 25.6 %reshape.256 = bf16[65536,128]{1,0:T(8,128)(2,1)} reshape(bf16[16,256,2048]{2,1,0:T(8,128)(2,1)} %param.18) | data formatting | bytes 33554432 | tf_op jit(solution)/shard_map/reshape | solution.py:102
  108.2 24.5 %reshape.246 = bf16[65536,128]{1,0:T(8,128)(2,1)} reshape(bf16[16,2048,256]{2,1,0:T(8,128)(2,1)} %param.19) | data formatting | bytes 33554432 | tf_op jit(solution)/shard_map/reshape | solution.py:102
  133.4 51.0 %scatter_custom_fusion.1 = bf16[65536,128]{1,0:T(8,128)(2,1)} fusion(bf16[65536,128]{1,0:T(8,128)(2,1)} %reshape.253, s32[640]{0:T(1024)S(1)} %get-tuple-element.6, f32[640,128]{1,0:T(8,128)S(1)} %fusion.10, pred[640]{0:T(1024)(128)(4,1)S(1)} %get-tuple-element.12, bf16[]{:T(256)} %constant.122.clone.3, s32[1024]{0:T(1024)S(1)} %get-tuple-element.18), kind=kCustom, calls=%fused_computation.50 | custom fusion | flops 327680 | bytes 33887232 | tf_op jit(solution)/shard_map/scatter | solution.py:110
  184.4 25.3 %reshape.319 = bf16[16,256,2048,1]{2,1,0,3:T(8,128)(2,1)} reshape(bf16[65536,128]{1,0:T(8,128)(2,1)} %scatter_custom_fusion.1) | data formatting | bytes 33554432 | tf_op jit(solution)/shard_map/reshape | solution.py:110
  209.7 50.1 %scatter_custom_fusion.2 = bf16[65536,128]{1,0:T(8,128)(2,1)} fusion(bf16[65536,128]{1,0:T(8,128)(2,1)} %reshape.256, s32[640]{0:T(1024)S(1)} %get-tuple-element.7, f32[640,128]{1,0:T(8,128)S(1)} %fusion.10, pred[640]{0:T(1024)(128)(4,1)S(1)} %get-tuple-element.13, bf16[]{:T(256)} %constant.122.clone.3, s32[1024]{0:T(1024)S(1)} %get-tuple-element.17), kind=kCustom, calls=%fused_computation.51 | custom fusion | flops 327680 | bytes 33887232 | tf_op jit(solution)/shard_map/scatter | solution.py:110
  259.8 25.3 %reshape.320 = bf16[16,256,2048,1]{2,1,0,3:T(8,128)(2,1)} reshape(bf16[65536,128]{1,0:T(8,128)(2,1)} %scatter_custom_fusion.2) | data formatting | bytes 33554432 | tf_op jit(solution)/shard_map/reshape | solution.py:110
  285.1 49.4 %scatter_custom_fusion = bf16[65536,128]{1,0:T(8,128)(2,1)} fusion(bf16[65536,128]{1,0:T(8,128)(2,1)} %reshape.246, s32[640]{0:T(1024)S(1)} %get-tuple-element.8, f32[640,128]{1,0:T(8,128)S(1)} %fusion.10, pred[640]{0:T(1024)(128)(4,1)S(1)} %get-tuple-element.14, bf16[]{:T(256)} %constant.122.clone.3, s32[1024]{0:T(1024)S(1)} %pad_clamp_fusion.2), kind=kCustom, calls=%fused_computation.49 | custom fusion | flops 327680 | bytes 33887232 | tf_op jit(solution)/shard_map/scatter | solution.py:110
  334.5 24.5 %reshape.321 = bf16[16,2048,256,1]{2,1,0,3:T(8,128)(2,1)} reshape(bf16[65536,128]{1,0:T(8,128)(2,1)} %scatter_custom_fusion) | data formatting | bytes 33554432 | tf_op jit(solution)/shard_map/reshape | solution.py:110
  359.0 10.9 %fusion.13 = f32[4,16,15,256]{3,2,0,1:T(8,128)S(1)} fusion(bf16[4,16,15,2048]{3,1,2,0:T(8,128)(2,1)} %all-to-all-done.2, bf16[16,256,2048,1]{2,1,0,3:T(8,128)(2,1)} %reshape.319), kind=kOutput, calls=%fused_computation.22 | convolution fusion | flops 1006632960 | bytes 21692416 | tf_op jit(solution)/shard_map/secd,efd->secf/dot_general | solution.py:132
  369.9 19.8 %convert_bitcast_fusion = bf16[4,16,15,2048]{3,2,0,1:T(8,128)(2,1)} fusion(bf16[16,2048,256,1]{2,1,0,3:T(8,128)(2,1)} %reshape.321, bf16[4,16,15,2048]{3,1,2,0:T(8,128)(2,1)} %all-to-all-done.2, bf16[16,256,2048,1]{2,1,0,3:T(8,128)(2,1)} %reshape.320, f32[4,16,15,256]{3,2,0,1:T(8,128)S(1)} %fusion.13), kind=kOutput, calls=%fused_computation.12 | convolution fusion | flops 2016706560 | bytes 42401792 | tf_op jit(solution)/shard_map/secf,edf->secd/dot_general | solution.py:136
  389.7 6.5 %copy.64 = bf16[4,16,15,2048]{3,1,2,0:T(8,128)(2,1)} copy(bf16[4,16,15,2048]{3,2,0,1:T(8,128)(2,1)} %convert_bitcast_fusion) | data formatting | bytes 7864320 | tf_op jit(solution)/shard_map/convert_element_type | solution.py:138
  396.2 16.1 %all-to-all-start.3 = ((bf16[4,16,15,2048]{3,1,2,0:T(8,128)(2,1)}), bf16[4,16,15,2048]{3,1,2,0:T(8,128)(2,1)}, u32[]{:S(2)}, u32[]{:S(2)}) async-start(bf16[4,16,15,2048]{3,1,2,0:T(8,128)(2,1)} %copy.64), calls=%async_computation.3 | async-start | bytes 7864320 | tf_op jit(solution)/shard_map/all_to_all | solution.py:139
  413.2 86.1 %all-to-all-done.3 = bf16[4,16,15,2048]{3,1,2,0:T(8,128)(2,1)} async-done(((bf16[4,16,15,2048]{3,1,2,0:T(8,128)(2,1)}), bf16[4,16,15,2048]{3,1,2,0:T(8,128)(2,1)}, u32[]{:S(2)}, u32[]{:S(2)}) %all-to-all-start.3) | async-done | bytes 3932192 | tf_op jit(solution)/shard_map/all_to_all | solution.py:139
  499.4 6.3 %copy.65 = bf16[4,16,15,2048]{3,2,1,0:T(8,128)(2,1)} copy(bf16[4,16,15,2048]{3,1,2,0:T(8,128)(2,1)} %all-to-all-done.3) | data formatting | bytes 7864320 | tf_op jit(solution)/shard_map/all_to_all | solution.py:139
  505.6 5.1 reshape.258
  510.7 4.9 convolution_convert_fusion.1
  515.7 19.9 %reduce-scatter.2.cloned.1.call-done = bf16[48,512]{1,0:T(8,128)(2,1)} async-done(((bf16[48,2048]{1,0:T(8,128)(2,1)}), bf16[48,512]{1,0:T(8,128)(2,1)}) %reduce-scatter.2.cloned.1.call-update) | async-done | bytes 49168 | tf_op jit(solution)/shard_map/reduce_scatter | solution.py:145
  (54 shorter events, 18.0 us)
Async XLA Ops:
  12.7 18.6 %all-to-all-start = ((s32[4,1,160]{2,1,0:T(1,128)}), s32[4,1,160]{2,1,0:T(1,128)S(1)}, u32[]{:S(2)}, u32[]{:S(2)}) async-start(s32[4,1,160]{2,1,0:T(1,128)} %all_to_all.15), calls=%async_computation | async-start | bytes 8192 | tf_op jit(solution)/shard_map/all_to_all | solution.py:92
  31.3 20.4 %all-to-all-start.1 = ((bf16[4,160,128]{2,1,0:T(8,128)(2,1)}), bf16[4,160,128]{2,1,0:T(8,128)(2,1)S(1)}, u32[]{:S(2)}, u32[]{:S(2)}) async-start(bf16[4,160,128]{2,1,0:T(8,128)(2,1)} %bitcast.10), calls=%async_computation.1 | async-start | bytes 327680 | tf_op jit(solution)/shard_map/all_to_all | solution.py:85
  51.7 307.2 %all-to-all-start.2 = ((bf16[4,16,15,2048]{3,1,2,0:T(8,128)(2,1)}), bf16[4,16,15,2048]{3,1,2,0:T(8,128)(2,1)}, u32[]{:S(2)}, u32[]{:S(2)}) async-start(bf16[4,16,15,2048]{3,1,2,0:T(8,128)(2,1)} %copy.61), calls=%async_computation.2 | async-start | bytes 7864320 | tf_op jit(solution)/shard_map/all_to_all | solution.py:131
  369.9 42.6 %copy-start = (f32[48,8]{0,1:T(8,128)S(1)}, f32[48,8]{0,1:T(8,128)}, u32[]{:S(2)}) copy-start(f32[48,8]{0,1:T(8,128)} %param.16) | copy-start | bytes 4612
  396.2 103.2 %all-to-all-start.3 = ((bf16[4,16,15,2048]{3,1,2,0:T(8,128)(2,1)}), bf16[4,16,15,2048]{3,1,2,0:T(8,128)(2,1)}, u32[]{:S(2)}, u32[]{:S(2)}) async-start(bf16[4,16,15,2048]{3,1,2,0:T(8,128)(2,1)} %copy.64), calls=%async_computation.3 | async-start | bytes 7864320 | tf_op jit(solution)/shard_map/all_to_all | solution.py:139
  412.3 123.3 %reduce-scatter.2.cloned.1.call-start = ((), (), s32[]{:S(2)}) async-start(), calls=%async_computation.5 | async-start | bytes 245760 | tf_op jit(solution)/shard_map/reduce_scatter | solution.py:145
Sparse Core Ops, SparseCore 0:
  515.8 19.7 reduce-scatter.1
where the time goes:
time: 553 us; the launch traced here: 543 us
  local copies, waits for them, and re-layouts  183 us (33%)
  other arithmetic  159 us (29%)
  waiting for transfers between devices  106 us (19%)
  matrix products  42.1 us (8%)
  starting transfers between devices  33.1 us (6%)
  between operations  14 us (3%)
  blocking collectives  5.8 us (1%)
    scatter x3, other arithmetic, updated(): flat_weight.at[row_index].set(new_rows, mode='drop').reshape(weight.shape)  150 us
    all_to_all x1, waiting for transfers between devices, per_device(): lax.all_to_all(partial_value, 'ep', split_axis=0, concat_axis=0, tiled=True)  86.1 us
    reshape x3, local copies, waits for them, and re-layouts, updated(): flat_weight = weight.reshape(-1, block)  75.7 us
    reshape x3, local copies, waits for them, and re-layouts, updated(): flat_weight.at[row_index].set(new_rows, mode='drop').reshape(weight.shape)  75 us
    reduce_scatter x1, waiting for transfers between devices, per_device(): lax.psum_scatter(weighted.astype(jnp.bfloat16), 'tp', scatter_dimension=1...  19.9 us
    dot_general x1, matrix products, per_device(): jnp.einsum('secf,edf->secd', hidden, new_down, preferred_element_type=jnp...  19.8 us
    all_to_all x1, starting transfers between devices, per_device(): lax.all_to_all(partial_value, 'ep', split_axis=0, concat_axis=0, tiled=True)  16.1 us
    reshape x2, local copies, waits for them, and re-layouts, per_device(): sending = sending.reshape(ep_count, exp_dev, CAP, feature_count)  11.5 us
  transfers between devices with their start and end apart: 5, of which 2 were waited for; matrix products, arithmetic and copies ran while one was open for 60% of the time, Pallas kernels for 0%

commit v1 on v0

--- a/solution.py
+++ b/solution.py
@@ -1,6 +1,10 @@
+import functools
+
 import jax
 import jax.numpy as jnp
 from jax import lax
+from jax.experimental import pallas as pl
+from jax.experimental.pallas import tpu as pltpu
 from jax.sharding import PartitionSpec as P
 
 EXPERTS = 64
@@ -17,7 +21,7 @@
     return (floats * scaling * gain).astype(jnp.bfloat16)
 
 
-def per_device(
+def routed(
     tokens,
     norm_gain,
     route_ids,
@@ -145,6 +149,214 @@
     return lax.psum_scatter(weighted.astype(jnp.bfloat16), "tp", scatter_dimension=1, tiled=True)
 
 
+MAX_ROWS = 512
+SUB = 1 << 15
+META_ROWS = 32
+
+
+def split_parts(whole):
+    high = whole.astype(jnp.bfloat16)
+    rest = whole - high.astype(jnp.float32)
+    middle = rest.astype(jnp.bfloat16)
+    low = (rest - middle.astype(jnp.float32)).astype(jnp.bfloat16)
+    return [high, middle, low]
+
+
+def expert_kernel(
+    table, begins, rank, tokens, gain, ids, shares, values, gate, up, down, out, normed, total
+):
+    step = pl.program_id(0)
+    exp_dev = pl.num_programs(0)
+    ep_count, tp_count, rows, part = tokens.shape
+    width = tp_count * part
+
+    @pl.when(step == 0)
+    def _():
+        for i in range(ep_count):
+            scale = jnp.zeros((rows, 1), jnp.float32)
+            for c in range(tp_count):
+                floats = tokens[i, c].astype(jnp.float32)
+                scale += jnp.sum(floats * floats, axis=1, keepdims=True)
+            scale = lax.rsqrt(scale / width + EPS)
+            for c in range(tp_count):
+                span = slice(c * part, (c + 1) * part)
+                normed[i * rows : (i + 1) * rows, span] = (
+                    tokens[i, c].astype(jnp.float32) * scale * gain[:, span]
+                ).astype(jnp.bfloat16)
+
+    line = lax.broadcasted_iota(jnp.int32, (16, 128), 0)
+    for m, weight in enumerate((gate, up, down)):
+
+        @pl.loop(begins[3 * step + m], begins[3 * step + m + 1])
+        def _(b):
+            place = table[b]
+            row, column = place // 16, place % 16
+            first = pl.multiple_of(row // 16 * 16, 16)
+            where = (0, pl.ds(first, 16), pl.ds(pl.multiple_of(column * 128, 128), 128))
+            added = jnp.where(line == row - first, values[pl.ds(b, 1), :], 0.0)
+            weight[where] = (weight[where].astype(jnp.float32) + added).astype(jnp.bfloat16)
+
+    dims = (((1,), (1,)), ((), ()))
+    share = jnp.sum(
+        jnp.where(ids[...] == rank[0] * exp_dev + step, shares[...], 0.0), axis=1, keepdims=True
+    )
+    gated = lax.dot_general(normed[...], gate[0], dims, preferred_element_type=jnp.float32)
+    upped = lax.dot_general(normed[...], up[0], dims, preferred_element_type=jnp.float32)
+    hidden = (gated / (1.0 + jnp.exp(-gated)) * upped * share).astype(jnp.bfloat16)
+
+    for c in range(tp_count):
+        span = slice(c * part, (c + 1) * part)
+        term = lax.dot_general(hidden, down[0, span, :], dims, preferred_element_type=jnp.float32)
+
+        @pl.when(step == 0)
+        def _():
+            total[:, span] = term
+
+        @pl.when(step > 0)
+        def _():
+            total[:, span] += term
+
+    @pl.when(step == exp_dev - 1)
+    def _():
+        for i in range(ep_count):
+            for c in range(tp_count):
+                out[i, c] = total[
+                    i * rows : (i + 1) * rows, c * part : (c + 1) * part
+                ].astype(jnp.bfloat16)
+
+
+def expert_sums(table, begins, rank, tokens, gain, ids, shares, values, gate, up, down):
+    ep_count, tp_count, rows, part = tokens.shape
+    exp_dev, ff_local, width = gate.shape
+
+    def held(array):
+        return pl.BlockSpec(array.shape, lambda step, *_: (0,) * array.ndim)
+
+    def one(array):
+        return pl.BlockSpec((1,) + array.shape[1:], lambda step, *_: (step, 0, 0))
+
+    return pl.pallas_call(
+        expert_kernel,
+        out_shape=jax.ShapeDtypeStruct(tokens.shape, jnp.bfloat16),
+        grid_spec=pltpu.PrefetchScalarGridSpec(
+            num_scalar_prefetch=3,
+            grid=(exp_dev,),
+            in_specs=[held(tokens), held(gain), held(ids), held(shares), held(values)]
+            + [one(gate), one(up), one(down)],
+            out_specs=held(tokens),
+            scratch_shapes=[
+                pltpu.VMEM((ep_count * rows, width), jnp.bfloat16),
+                pltpu.VMEM((ep_count * rows, width), jnp.float32),
+            ],
+        ),
+        compiler_params=pltpu.CompilerParams(vmem_limit_bytes=40 << 20),
+    )(table, begins, rank, tokens, gain, ids, shares, values, gate, up, down)
+
+
+def sorted_updates(owned, placing, values, ep_count, exp_dev, ff_local, width, limit):
+    block = values.shape[1]
+    count = values.shape[0]
+    learner = jnp.arange(count, dtype=jnp.int32) // (count // ep_count)
+    per_row, per_down = width // block, ff_local // block
+    ff_rows, d_rows = ff_local // ep_count, width // ep_count
+    span = ff_rows * per_row
+    places = 2 * span + d_rows * per_down
+    spot = placing % places
+    matrix = jnp.minimum(spot // span, 2)
+    remain = spot - matrix * span
+    row_up, column_up = learner * ff_rows + remain // per_row, remain % per_row
+    row_down, column_down = learner * d_rows + remain // per_down, remain % per_down
+    row = jnp.where(matrix == 2, row_down, row_up)
+    column = jnp.where(matrix == 2, column_down, column_up)
+    target = (placing // places * 3 + matrix) * SUB + row * 16 + column
+    target = jnp.where(owned, target, 1 << 30)
+    order = jnp.arange(count, dtype=jnp.int32)
+    ahead = jnp.logical_or(
+        target[None, :] < target[:, None],
+        jnp.logical_and(target[None, :] == target[:, None], order[None, :] < order[:, None]),
+    )
+    position = jnp.sum(ahead.astype(jnp.int32), axis=1)
+    chosen = position[None, :] == jnp.arange(limit, dtype=jnp.int32)[:, None]
+    ordered = jnp.sum(jnp.where(chosen, target[None, :], 0), axis=1)
+    same = (ordered[:, None] == target[None, :]).astype(jnp.bfloat16)
+    combined = jnp.dot(same, values, preferred_element_type=jnp.float32)
+    repeated = jnp.concatenate([jnp.zeros((1,), jnp.bool_), ordered[1:] == ordered[:-1]])
+    combined = jnp.where(repeated[:, None], 0.0, combined)
+    edges = jnp.arange(3 * exp_dev + 1, dtype=jnp.int32) * SUB
+    begins = jnp.sum((target[None, :] < edges[:, None]).astype(jnp.int32), axis=1)
+    return ordered % SUB, begins, combined
+
+
+def gathered(
+    tokens,
+    norm_gain,
+    route_ids,
+    route_scores,
+    gate_weight,
+    up_weight,
+    down_weight,
+    delta_codes,
+    delta_exps,
+    delta_owner,
+    delta_places,
+):
+    ep_count, tp_count = lax.axis_size("ep"), lax.axis_size("tp")
+    ep_rank = lax.axis_index("ep")
+    exp_dev, ff_local, width = gate_weight.shape
+    block_count, block = delta_codes.shape[2:]
+    rows = tokens.shape[0]
+    limit = block_count * 5 // (2 * ep_count) * ep_count
+
+    delta_values = (
+        delta_codes[0, 0].astype(jnp.float32)
+        * jnp.exp2(delta_exps[0, 0].astype(jnp.float32))[:, None]
+    ).astype(jnp.bfloat16)
+    placing = delta_places[0, 0]
+    shares = route_scores / jnp.sum(route_scores, axis=1, keepdims=True)
+    numbers = [delta_owner[0, 0, :, 0], placing // 256, placing % 256]
+    meta = jnp.concatenate(
+        [number.astype(jnp.bfloat16) for number in numbers]
+        + [route_ids.reshape(-1).astype(jnp.bfloat16)]
+        + split_parts(shares.reshape(-1))
+    )
+    meta = jnp.pad(meta, (0, META_ROWS * block - meta.shape[0])).reshape(META_ROWS, block)
+    got = lax.all_gather(jnp.concatenate([delta_values, meta]), "ep")
+    got_tokens = lax.all_gather(tokens, ("ep", "tp"))
+
+    got_values = got[:, :block_count].reshape(-1, block)
+    got_meta = got[:, block_count:].reshape(ep_count, -1)
+    listed = got_meta[:, : 3 * block_count].reshape(ep_count, 3, block_count).astype(jnp.int32)
+    owner, high, low = (listed[:, k].reshape(-1) for k in range(3))
+    start, picks = 3 * block_count, rows * TOP
+    pieces = got_meta[:, start : start + 4 * picks].reshape(ep_count, 4, picks).astype(jnp.float32)
+    ids = pieces[:, 0].astype(jnp.int32).reshape(-1, TOP)
+    all_shares = (pieces[:, 1] + pieces[:, 2] + pieces[:, 3]).reshape(-1, TOP)
+    table, begins, values = sorted_updates(
+        owner == ep_rank, high * 256 + low, got_values, ep_count, exp_dev, ff_local, width, limit
+    )
+    sums = expert_sums(
+        table,
+        begins,
+        ep_rank.reshape(1).astype(jnp.int32),
+        got_tokens.reshape((ep_count, tp_count) + tokens.shape),
+        norm_gain.reshape(1, -1),
+        ids,
+        all_shares,
+        values,
+        gate_weight,
+        up_weight,
+        down_weight,
+    )
+    return lax.psum_scatter(
+        sums.reshape((ep_count * tp_count,) + tokens.shape), ("ep", "tp"), scatter_dimension=0
+    )
+
+
+def per_device(*args):
+    few = args[0].shape[0] * lax.axis_size("ep") <= MAX_ROWS
+    return gathered(*args) if few else routed(*args)
+
+
 def solution(mesh):
     placed = (
         P(("groups", "ep"), "tp"),

time: 553 us -> 166 us (0.30); the launches traced: 543 us -> 167 us
  local copies, waits for them, and re-layouts: 183 us -> 2.16 us
  other arithmetic: 159 us -> 6.73 us
  matrix products: 42.1 us -> 0.56 us
  waiting for transfers between devices: 106 us -> 65 us
  Pallas kernels: 0 us -> 38.4 us
  blocking collectives: 5.8 us -> 40.2 us
  starting transfers between devices: 33.1 us -> 0.01 us
    reshape x11 -> x2, local copies, waits for them, and re-layouts: 167 us -> 0.1 us  [the longest x1 0.09 us: gathered(): shares.reshape(-1)]
    scatter x3 -> x0, other arithmetic: 150 us -> none  [updated(): flat_weight.at[row_index].set(new_rows, mode='drop').reshape(weight.shape)]
    all_to_all x4 -> x0, waiting for transfers between devices: 86.2 us -> none  [the longest x1 86.1 us: per_device(): lax.all_to_all(partial_value, 'ep', split_axis=0, concat_axis=0, tiled=True)]
    reduce_scatter x1, waiting for transfers between devices: 19.9 us -> 65 us  [gathered(): lax.psum_scatter(sums.reshape((ep_count * tp_count,) + tokens.shape), ('e...]
    dot_general x7 -> x1, matrix products: 42.1 us -> 0.56 us  [sorted_updates(): combined = jnp.dot(same, values, preferred_element_type=jnp.float32)]
    pallas_call x0 -> x1, Pallas kernels: none -> 38.4 us  [expert_sums(): pl.pallas_call(expert_kernel, out_shape=jax.ShapeDtypeStruct(tokens.shape...]
    all_gather x1 -> x2, blocking collectives: 5.8 us -> 40.2 us  [the longest x1 24.6 us: gathered(): got_tokens = lax.all_gather(tokens, ('ep', 'tp'))]
    all_to_all x4 -> x0, starting transfers between devices: 32.8 us -> none  [the longest x1 16.1 us: per_device(): lax.all_to_all(partial_value, 'ep', split_axis=0, concat_axis=0, tiled=True)]
  transfers between devices with their start and end apart: 5 -> 1, of which waited for: 2 -> 1; matrix products, arithmetic and copies ran while one was open for 60% -> 0% of each run, Pallas kernels for 0% -> 0%
where the time goes in v1:
time: 166 us; the launch traced here: 167 us
  waiting for transfers between devices  65 us (39%)
  blocking collectives  40.2 us (24%)
  Pallas kernels  38.4 us (23%)
  between operations  13.5 us (8%)
  other arithmetic  6.73 us (4%)
  local copies, waits for them, and re-layouts  2.16 us (1%)
    reduce_scatter x1, waiting for transfers between devices, gathered(): lax.psum_scatter(sums.reshape((ep_count * tp_count,) + tokens.shape), ('e...  65 us
    pallas_call x1, Pallas kernels, expert_sums(): pl.pallas_call(expert_kernel, out_shape=jax.ShapeDtypeStruct(tokens.shape...  38.4 us
    all_gather x1, blocking collectives, gathered(): got_tokens = lax.all_gather(tokens, ('ep', 'tp'))  24.6 us
    all_gather x1, blocking collectives, gathered(): got = lax.all_gather(jnp.concatenate([delta_values, meta]), 'ep')  15.6 us
  transfers between devices with their start and end apart: 1, of which 1 were waited for; matrix products, arithmetic and copies ran while one was open for 0% of the time, Pallas kernels for 0%

profile of v1, /device:TPU:0, one launch (start us, length us, event | category | flops | bytes accessed | tf_op | source)
XLA Modules:
  0.0 166.6 jit_solution(3887225341491831060)
XLA Ops:
  6.5 0.7 convert_reduce_fusion.2
  7.2 0.7 multiply_exponential_fusion
  7.9 0.7 fusion.37
  8.6 0.7 convert_element_type.86
  9.3 0.7 reduce_sum.36
  10.0 0.7 broadcast_divide_fusion
  10.8 0.1 convert_element_type.87
  11.1 0.2 dynamic-update-slice
  11.3 0.2 dynamic-update-slice.1
  11.6 0.2 dynamic-update-slice.2
  11.8 0.2 dynamic-update-slice.3
  12.0 0.2 dynamic-update-slice.4
  12.2 0.2 dynamic-update-slice.5
  12.4 0.2 dynamic-update-slice.6
  12.6 0.9 fusion.9
  13.6 15.6 %all-gather = bf16[1152,128]{1,0:T(8,128)(2,1)S(1)} all-gather(bf16[288,128]{1,0:T(8,128)(2,1)S(1)} %pad_maximum_fusion), channel_id=2, replica_groups=mesh['groups'=2,'ep'=4,'tp'=4] {'ep'}, dimensions={0}, use_global_device_ids=true | all-gather | bytes 368640 | tf_op jit(solution)/shard_map/all_gather | solution.py:323
  29.4 0.8 convert_reduce_fusion
  30.3 0.3 select_reduce_fusion
  30.7 0.2 convert_reduce_fusion.1.begins
  30.9 0.1 add.192.shares
  31.1 24.6 %all-gather.1 = bf16[768,512]{1,0:T(8,128)(2,1)S(1)} all-gather(bf16[48,512]{1,0:T(8,128)(2,1)} %param.11), channel_id=3, replica_groups=mesh['groups'=2,'ep'=4,'tp'=4] {'ep','tp'}, dimensions={0}, use_global_device_ids=true | all-gather | bytes 835584 | tf_op jit(solution)/shard_map/all_gather | solution.py:324
  55.8 0.6 fusion.6.values
  56.3 38.4 %shard_map.109 = bf16[4,4,48,512]{3,2,1,0:T(8,128)(2,1)} custom-call(s32[640]{0:T(1024)S(1)} %add_select_fusion.table, s32[49]{0:T(128)S(1)} %convert_reduce_fusion.1.begins, s32[1]{0:T(128)} %bitcast.7.rank, bf16[4,4,48,512]{3,2,1,0:T(8,128)(2,1)S(1)} %bitcast.40, f32[1,2048]{1,0:T(1,128)S(1)} %bitcast.41, s32[192,8]{1,0:T(8,128)S(1)} %convert_element_type.100.ids, ...), custom_call_target="tpu_custom_call" | custom-call | tf_op jit(solution)/shard_map/pallas_call | solution.py:238
  94.8 65.0 %reduce-scatter.2.cloned.1.call-done = bf16[1,48,512]{2,1,0:T(8,128)(2,1)} async-done(((bf16[16,48,512]{2,1,0:T(8,128)(2,1)}), bf16[1,48,512]{2,1,0:T(8,128)(2,1)}) %reduce-scatter.2.cloned.1.call-update) | async-done | bytes 49168 | tf_op jit(solution)/shard_map/reduce_scatter | solution.py:350
  (31 shorter events, 0.7 us)
Async XLA Ops:
  6.5 49.8 %copy-start = (f32[2048]{0:T(1024)S(1)}, f32[2048]{0:T(1024)}, u32[]{:S(2)}) copy-start(f32[2048]{0:T(1024)} %param.12) | copy-start | bytes 24580
  6.5 153.2 %reduce-scatter.2.cloned.1.call-start = ((), (), s32[]{:S(2)}) async-start(), calls=%async_computation.1 | async-start | bytes 835584 | tf_op jit(solution)/shard_map/reduce_scatter | solution.py:350
Sparse Core Ops, SparseCore 0:
  94.9 64.7 reduce-scatter.1

commit v2 on v1

--- a/solution.py
+++ b/solution.py
@@ -151,23 +151,178 @@
 
 MAX_ROWS = 512
 SUB = 1 << 15
-META_ROWS = 32
-
-
-def split_parts(whole):
-    high = whole.astype(jnp.bfloat16)
-    rest = whole - high.astype(jnp.float32)
-    middle = rest.astype(jnp.bfloat16)
-    low = (rest - middle.astype(jnp.float32)).astype(jnp.bfloat16)
-    return [high, middle, low]
+NOTE_ROWS = 16
+MESH = pl.DeviceIdType.MESH
+
+
+def partners():
+    z, c = lax.axis_index("ep"), lax.axis_index("tp")
+    return z, c, lax.rem(c + 2, 4), c + 1 - 2 * lax.rem(c, 2)
+
+
+def greet(z, far, near, ep_count):
+    barrier = pltpu.get_barrier_semaphore()
+    for k in range(1, ep_count):
+        pl.semaphore_signal(
+            barrier, inc=1, device_id={"ep": lax.rem(z + k, ep_count)}, device_id_type=MESH
+        )
+    for other in (far, near):
+        pl.semaphore_signal(barrier, inc=1, device_id={"tp": other}, device_id_type=MESH)
+    pl.semaphore_wait(barrier, ep_count + 1)
+
+
+def send(source, target, send_sem, recv_sem, device):
+    copy = pltpu.make_async_remote_copy(
+        src_ref=source,
+        dst_ref=target,
+        send_sem=send_sem,
+        recv_sem=recv_sem,
+        device_id=device,
+        device_id_type=MESH,
+    )
+    copy.start()
+    return copy
+
+
+def gather_kernel(tokens, codes, notes, all_tokens, all_codes, all_notes, sent, came, own_sem):
+    ep_count = all_tokens.shape[1]
+    z, c, far, near = partners()
+    own = []
+    for i, (mine, slot) in enumerate(
+        ((tokens, all_tokens.at[c, z]), (codes, all_codes.at[z]), (notes, all_notes.at[z]))
+    ):
+        copy = pltpu.make_async_copy(mine, slot, own_sem.at[i])
+        copy.start()
+        own.append(copy)
+    greet(z, far, near, ep_count)
+    others = range(1, ep_count)
+    used = iter(range(sent.shape[0]))
+
+    def launch(source, target, device):
+        at = next(used)
+        return send(source, target, sent.at[at], came.at[at], device)
+
+    def peer(k):
+        return {"ep": lax.rem(z + k, ep_count)}
+
+    told = [launch(notes, all_notes.at[z], peer(k)) for k in others]
+    rows = [launch(tokens, all_tokens.at[c, z], peer(k)) for k in others]
+    slot = all_tokens.at[c, z]
+    across = [launch(tokens, slot, {"tp": far})]
+    beside = [launch(tokens, slot, {"tp": near})]
+    blocks = [launch(codes, all_codes.at[z], peer(k)) for k in others]
+    for k in others:
+        rows[k - 1].wait_recv()
+        slot = all_tokens.at[c, lax.rem(z + ep_count - k, ep_count)]
+        across.append(launch(slot, slot, {"tp": far}))
+        beside.append(launch(slot, slot, {"tp": near}))
+    for k in range(ep_count):
+        across[k].wait_recv()
+        slot = all_tokens.at[far, lax.rem(z + ep_count - k, ep_count)]
+        beside.append(launch(slot, slot, {"tp": near}))
+    for copy in told + blocks + beside:
+        copy.wait_recv()
+    for copy in told + blocks + beside + rows + across:
+        copy.wait_send()
+    for copy in own:
+        copy.wait()
+
+
+def gather(tokens, codes, notes, ep_count, tp_count):
+    copies = 3 * (ep_count - 1) + 3 * ep_count
+    vmem = pl.BlockSpec(memory_space=pltpu.VMEM)
+    return pl.pallas_call(
+        gather_kernel,
+        out_shape=[
+            jax.ShapeDtypeStruct((tp_count, ep_count) + tokens.shape, tokens.dtype),
+            jax.ShapeDtypeStruct((ep_count,) + codes.shape, codes.dtype),
+            jax.ShapeDtypeStruct((ep_count,) + notes.shape, notes.dtype),
+        ],
+        in_specs=[vmem] * 3,
+        out_specs=[vmem] * 3,
+        scratch_shapes=[
+            pltpu.SemaphoreType.DMA((copies,)),
+            pltpu.SemaphoreType.DMA((copies,)),
+            pltpu.SemaphoreType.DMA((3,)),
+        ],
+        compiler_params=pltpu.CompilerParams(
+            collective_id=0, has_side_effects=True, vmem_limit_bytes=16 << 20
+        ),
+    )(tokens, codes, notes)
+
+
+def scatter_kernel(
+    sums, out, first, second, third, to_far, to_peer, sent, came
+):
+    ep_count = sums.shape[1]
+    z, c, far, near = partners()
+    beyond = far + 1 - 2 * lax.rem(far, 2)
+    greet(z, far, near, ep_count)
+    used = iter(range(sent.shape[0]))
+
+    def launch(source, target, device):
+        at = next(used)
+        return send(source, target, sent.at[at], came.at[at], device)
+
+    order = [lax.rem(z + k, ep_count) for k in list(range(1, ep_count)) + [0]]
+    relayed = [launch(sums.at[beyond, j], first.at[0, j], {"tp": near}) for j in order]
+    direct = [launch(sums.at[near, j], first.at[1, j], {"tp": near}) for j in order]
+
+    def wide(block):
+        return block.astype(jnp.float32)
+
+    across = []
+    for copy, j in zip(relayed, order):
+        copy.wait_recv()
+        to_far[j] = (wide(sums[far, j]) + wide(first[0, j])).astype(jnp.bfloat16)
+        across.append(launch(to_far.at[j], second.at[j], {"tp": far}))
+    peers = []
+    for k, j in enumerate(order):
+        direct[k].wait_recv()
+        across[k].wait_recv()
+        summed = wide(sums[c, j]) + wide(first[1, j]) + wide(second[j])
+        if k < ep_count - 1:
+            to_peer[k] = summed.astype(jnp.bfloat16)
+            peers.append(launch(to_peer.at[k], third.at[k], {"ep": j}))
+    for k, copy in enumerate(peers):
+        copy.wait_recv()
+        summed = summed + wide(third[k])
+    out[...] = summed.astype(jnp.bfloat16)
+    for copy in relayed + direct + across + peers:
+        copy.wait_send()
+
+
+def scatter_sums(sums):
+    tp_count, ep_count = sums.shape[:2]
+    block = sums.shape[2:]
+    copies = 4 * ep_count - 1
+    vmem = pl.BlockSpec(memory_space=pltpu.VMEM)
+    return pl.pallas_call(
+        scatter_kernel,
+        out_shape=jax.ShapeDtypeStruct(block, jnp.bfloat16),
+        in_specs=[vmem],
+        out_specs=vmem,
+        scratch_shapes=[
+            pltpu.VMEM((2, ep_count) + block, jnp.bfloat16),
+            pltpu.VMEM((ep_count,) + block, jnp.bfloat16),
+            pltpu.VMEM((ep_count - 1,) + block, jnp.bfloat16),
+            pltpu.VMEM((ep_count,) + block, jnp.bfloat16),
+            pltpu.VMEM((ep_count - 1,) + block, jnp.bfloat16),
+            pltpu.SemaphoreType.DMA((copies,)),
+            pltpu.SemaphoreType.DMA((copies,)),
+        ],
+        compiler_params=pltpu.CompilerParams(
+            collective_id=1, has_side_effects=True, vmem_limit_bytes=16 << 20
+        ),
+    )(sums)
 
 
 def expert_kernel(
-    table, begins, rank, tokens, gain, ids, shares, values, gate, up, down, out, normed, total
+    table, begins, rank, tokens, gain, ids, scores, values, gate, up, down, out, normed, total
 ):
     step = pl.program_id(0)
     exp_dev = pl.num_programs(0)
-    ep_count, tp_count, rows, part = tokens.shape
+    tp_count, ep_count, rows, part = tokens.shape
     width = tp_count * part
 
     @pl.when(step == 0)
@@ -175,58 +330,53 @@
         for i in range(ep_count):
             scale = jnp.zeros((rows, 1), jnp.float32)
             for c in range(tp_count):
-                floats = tokens[i, c].astype(jnp.float32)
+                floats = tokens[c, i].astype(jnp.float32)
                 scale += jnp.sum(floats * floats, axis=1, keepdims=True)
             scale = lax.rsqrt(scale / width + EPS)
             for c in range(tp_count):
                 span = slice(c * part, (c + 1) * part)
-                normed[i * rows : (i + 1) * rows, span] = (
-                    tokens[i, c].astype(jnp.float32) * scale * gain[:, span]
-                ).astype(jnp.bfloat16)
+                total[span, i * rows : (i + 1) * rows] = (
+                    tokens[c, i].astype(jnp.float32) * scale * gain[:, span]
+                ).T
+        normed[...] = total[...].astype(jnp.bfloat16)
+        total[...] = jnp.zeros_like(total)
 
     line = lax.broadcasted_iota(jnp.int32, (16, 128), 0)
-    for m, weight in enumerate((gate, up, down)):
-
-        @pl.loop(begins[3 * step + m], begins[3 * step + m + 1])
-        def _(b):
-            place = table[b]
+    starts = [begins[3 * step + m] for m in range(3)]
+    counts = [begins[3 * step + m + 1] - starts[m] for m in range(3)]
+
+    @pl.loop(0, jnp.maximum(jnp.maximum(counts[0], counts[1]), counts[2]))
+    def _(n):
+        for m, weight in enumerate((gate, up, down)):
+            valid = n < counts[m]
+            b = jnp.where(valid, starts[m] + n, 0)
+            place = jnp.where(valid, table[b], 0)
             row, column = place // 16, place % 16
             first = pl.multiple_of(row // 16 * 16, 16)
             where = (0, pl.ds(first, 16), pl.ds(pl.multiple_of(column * 128, 128), 128))
-            added = jnp.where(line == row - first, values[pl.ds(b, 1), :], 0.0)
+            at = jnp.where(valid, row - first, -1)
+            added = jnp.where(line == at, values[pl.ds(b, 1), :], 0.0)
             weight[where] = (weight[where].astype(jnp.float32) + added).astype(jnp.bfloat16)
 
-    dims = (((1,), (1,)), ((), ()))
-    share = jnp.sum(
-        jnp.where(ids[...] == rank[0] * exp_dev + step, shares[...], 0.0), axis=1, keepdims=True
-    )
-    gated = lax.dot_general(normed[...], gate[0], dims, preferred_element_type=jnp.float32)
-    upped = lax.dot_general(normed[...], up[0], dims, preferred_element_type=jnp.float32)
+    picked = jnp.where(ids[...] == rank[0] * exp_dev + step, scores[...], 0.0)
+    share = jnp.sum(picked, axis=0, keepdims=True) / jnp.sum(scores[...], axis=0, keepdims=True)
+    gated = jnp.dot(gate[0], normed[...], preferred_element_type=jnp.float32)
+    upped = jnp.dot(up[0], normed[...], preferred_element_type=jnp.float32)
     hidden = (gated / (1.0 + jnp.exp(-gated)) * upped * share).astype(jnp.bfloat16)
-
     for c in range(tp_count):
         span = slice(c * part, (c + 1) * part)
-        term = lax.dot_general(hidden, down[0, span, :], dims, preferred_element_type=jnp.float32)
-
-        @pl.when(step == 0)
-        def _():
-            total[:, span] = term
-
-        @pl.when(step > 0)
-        def _():
-            total[:, span] += term
+        total[span, :] += jnp.dot(down[0, span, :], hidden, preferred_element_type=jnp.float32)
 
     @pl.when(step == exp_dev - 1)
     def _():
-        for i in range(ep_count):
-            for c in range(tp_count):
-                out[i, c] = total[
-                    i * rows : (i + 1) * rows, c * part : (c + 1) * part
-                ].astype(jnp.bfloat16)
-
-
-def expert_sums(table, begins, rank, tokens, gain, ids, shares, values, gate, up, down):
-    ep_count, tp_count, rows, part = tokens.shape
+        for c in range(tp_count):
+            turned = total[c * part : (c + 1) * part, :].T
+            for i in range(ep_count):
+                out[c, i] = turned[i * rows : (i + 1) * rows, :].astype(jnp.bfloat16)
+
+
+def expert_sums(table, begins, rank, tokens, gain, ids, scores, values, gate, up, down):
+    tp_count, ep_count, rows, part = tokens.shape
     exp_dev, ff_local, width = gate.shape
 
     def held(array):
@@ -241,16 +391,16 @@
         grid_spec=pltpu.PrefetchScalarGridSpec(
             num_scalar_prefetch=3,
             grid=(exp_dev,),
-            in_specs=[held(tokens), held(gain), held(ids), held(shares), held(values)]
+            in_specs=[held(tokens), held(gain), held(ids.T), held(scores.T), held(values)]
             + [one(gate), one(up), one(down)],
             out_specs=held(tokens),
             scratch_shapes=[
-                pltpu.VMEM((ep_count * rows, width), jnp.bfloat16),
-                pltpu.VMEM((ep_count * rows, width), jnp.float32),
+                pltpu.VMEM((width, ep_count * rows), jnp.bfloat16),
+                pltpu.VMEM((width, ep_count * rows), jnp.float32),
             ],
         ),
         compiler_params=pltpu.CompilerParams(vmem_limit_bytes=40 << 20),
-    )(table, begins, rank, tokens, gain, ids, shares, values, gate, up, down)
+    )(table, begins, rank, tokens, gain, ids.T, scores.T, values, gate, up, down)
 
 
 def sorted_updates(owned, placing, values, ep_count, exp_dev, ff_local, width, limit):
@@ -307,53 +457,45 @@
     rows = tokens.shape[0]
     limit = block_count * 5 // (2 * ep_count) * ep_count
 
-    delta_values = (
-        delta_codes[0, 0].astype(jnp.float32)
-        * jnp.exp2(delta_exps[0, 0].astype(jnp.float32))[:, None]
-    ).astype(jnp.bfloat16)
-    placing = delta_places[0, 0]
-    shares = route_scores / jnp.sum(route_scores, axis=1, keepdims=True)
-    numbers = [delta_owner[0, 0, :, 0], placing // 256, placing % 256]
-    meta = jnp.concatenate(
-        [number.astype(jnp.bfloat16) for number in numbers]
-        + [route_ids.reshape(-1).astype(jnp.bfloat16)]
-        + split_parts(shares.reshape(-1))
-    )
-    meta = jnp.pad(meta, (0, META_ROWS * block - meta.shape[0])).reshape(META_ROWS, block)
-    got = lax.all_gather(jnp.concatenate([delta_values, meta]), "ep")
-    got_tokens = lax.all_gather(tokens, ("ep", "tp"))
-
-    got_values = got[:, :block_count].reshape(-1, block)
-    got_meta = got[:, block_count:].reshape(ep_count, -1)
-    listed = got_meta[:, : 3 * block_count].reshape(ep_count, 3, block_count).astype(jnp.int32)
-    owner, high, low = (listed[:, k].reshape(-1) for k in range(3))
-    start, picks = 3 * block_count, rows * TOP
-    pieces = got_meta[:, start : start + 4 * picks].reshape(ep_count, 4, picks).astype(jnp.float32)
-    ids = pieces[:, 0].astype(jnp.int32).reshape(-1, TOP)
-    all_shares = (pieces[:, 1] + pieces[:, 2] + pieces[:, 3]).reshape(-1, TOP)
+    numbers = [delta_exps, delta_owner, delta_places, route_ids, route_scores]
+    notes = jnp.concatenate([number.astype(jnp.float32).reshape(-1) for number in numbers])
+    notes = jnp.pad(notes, (0, NOTE_ROWS * block - notes.shape[0])).reshape(NOTE_ROWS, block)
+    got_tokens, got_codes, got_notes = gather(
+        tokens, delta_codes[0, 0], notes, ep_count, tp_count
+    )
+    got_notes = got_notes.reshape(ep_count, -1)
+    picks = rows * TOP
+    cuts = [0, block_count, 2 * block_count, 3 * block_count]
+    cuts += [cuts[3] + picks, cuts[3] + 2 * picks]
+    exps, owner, placing, ids, scores = (
+        got_notes[:, cuts[k] : cuts[k + 1]].reshape(-1) for k in range(5)
+    )
+    owner, placing = owner.astype(jnp.int32), placing.astype(jnp.int32)
+    ids = ids.astype(jnp.int32).reshape(-1, TOP)
+    scores = scores.reshape(-1, TOP)
+    got_values = got_codes.reshape(-1, block).astype(jnp.float32) * jnp.exp2(exps)[:, None]
+    got_values = got_values.astype(jnp.bfloat16)
     table, begins, values = sorted_updates(
-        owner == ep_rank, high * 256 + low, got_values, ep_count, exp_dev, ff_local, width, limit
+        owner == ep_rank, placing, got_values, ep_count, exp_dev, ff_local, width, limit
     )
     sums = expert_sums(
         table,
         begins,
         ep_rank.reshape(1).astype(jnp.int32),
-        got_tokens.reshape((ep_count, tp_count) + tokens.shape),
+        got_tokens,
         norm_gain.reshape(1, -1),
         ids,
-        all_shares,
+        scores,
         values,
         gate_weight,
         up_weight,
         down_weight,
     )
-    return lax.psum_scatter(
-        sums.reshape((ep_count * tp_count,) + tokens.shape), ("ep", "tp"), scatter_dimension=0
-    )
+    return scatter_sums(sums)
 
 
 def per_device(*args):
-    few = args[0].shape[0] * lax.axis_size("ep") <= MAX_ROWS
+    few = args[0].shape[0] * lax.axis_size("ep") <= MAX_ROWS and lax.axis_size("tp") == 4
     return gathered(*args) if few else routed(*args)
 
 

time: 166 us -> 77.6 us (0.47)
  waiting for transfers between devices: 65 us -> 0 us
  blocking collectives: 40.2 us -> 0 us
  Pallas kernels: 38.4 us -> 67.3 us
  between operations: 13.5 us -> 0.15 us
  other arithmetic: 6.73 us -> 4.35 us
  local copies, waits for them, and re-layouts: 2.16 us -> 4.41 us
    reduce_scatter x1 -> x0, waiting for transfers between devices: 65 us -> none  [gathered(): lax.psum_scatter(sums.reshape((ep_count * tp_count,) + tokens.shape), ('e...]
    all_gather x2 -> x0, blocking collectives: 40.2 us -> none  [the longest x1 24.6 us: gathered(): got_tokens = lax.all_gather(tokens, ('ep', 'tp'))]
    pallas_call x0 -> x2, Pallas kernels: none -> 36.6 us  [the longest x1 18.4 us: gather(): pl.pallas_call(gather_kernel, out_shape=[jax.ShapeDtypeStruct((tp_count,...]
    pallas_call x1, Pallas kernels: 38.4 us -> 30.7 us  [expert_sums(): pl.pallas_call(expert_kernel, out_shape=jax.ShapeDtypeStruct(tokens.shape...]
    unnamed x12 -> x16, local copies, waits for them, and re-layouts: 1.31 us -> 3.79 us
  transfers between devices with their start and end apart: 1 -> 0, of which waited for: 1 -> 0; matrix products, arithmetic and copies ran while one was open for 0% -> 0% of each run, Pallas kernels for 0% -> 0%
where the time goes in v2:
time: 77.6 us; the launch traced here: 76.9 us
  Pallas kernels  67.3 us (87%)
  local copies, waits for them, and re-layouts  4.41 us (6%)
  other arithmetic  4.35 us (6%)
    pallas_call x1, Pallas kernels, expert_sums(): pl.pallas_call(expert_kernel, out_shape=jax.ShapeDtypeStruct(tokens.shape...  30.7 us
    pallas_call x1, Pallas kernels, gather(): pl.pallas_call(gather_kernel, out_shape=[jax.ShapeDtypeStruct((tp_count,...  18.4 us
    pallas_call x1, Pallas kernels, scatter_sums(): pl.pallas_call(scatter_kernel, out_shape=jax.ShapeDtypeStruct(block, jnp....  18.2 us
    unnamed x16, local copies, waits for them, and re-layouts  3.79 us
    convert_element_type x4, other arithmetic, gathered(): number.astype(jnp.float32).reshape(-1)  2.73 us

profile of v2, /device:TPU:0, one launch (start us, length us, event | category | flops | bytes accessed | tf_op | source)
XLA Modules:
  0.0 76.9 jit_solution(4268433146414373070)
XLA Ops:
  0.0 0.7 convert_element_type.61
  0.7 0.7 convert_element_type.62
  1.4 0.7 convert_element_type.63
  2.0 0.7 convert_element_type.64
  2.8 0.1 copy.16
  2.8 0.1 reshape.297
  2.9 0.8 copy.17
  3.7 0.1 reshape.298
  3.8 0.8 %copy-done = bf16[1,1,256,128]{3,2,1,0:T(8,128)(2,1)S(1)} copy-done((bf16[1,1,256,128]{3,2,1,0:T(8,128)(2,1)S(1)}, bf16[1,1,256,128]{3,2,1,0:T(8,128)(2,1)}, u32[]{:S(2)}) %copy-start) | copy-done | bytes 65560
  4.7 0.8 %copy-done.1 = bf16[48,512]{1,0:T(8,128)(2,1)S(1)} copy-done((bf16[48,512]{1,0:T(8,128)(2,1)S(1)}, bf16[48,512]{1,0:T(8,128)(2,1)}, u32[]{:S(2)}) %copy-start.1) | copy-done | bytes 49176
  5.5 18.4 %shard_map.109 = (bf16[4,4,48,512]{3,2,1,0:T(8,128)(2,1)S(1)}, bf16[4,256,128]{2,1,0:T(8,128)(2,1)S(1)}, f32[4,16,128]{2,1,0:T(8,128)S(1)}) custom-call(bf16[48,512]{1,0:T(8,128)(2,1)S(1)} %copy-done.1, bf16[256,128]{1,0:T(8,128)(2,1)S(1)} %bitcast.25, f32[16,128]{1,0:T(8,128)S(1)} %pad_bitcast_fusion.notes), custom_call_target="tpu_custom_call" | custom-call | tf_op jit(solution)/shard_map/pallas_call | solution.py:234
  24.0 0.2 convert_reduce_fusion.1.begins
  24.2 0.9 %convert_reduce_fusion = s32[1024]{0:T(1024)S(1)} fusion(s32[1024]{0:T(1024)S(1)} %fusion.17), kind=kLoop, calls=%fused_computation | loop fusion | flops 7339008 | bytes 8192 | tf_op jit(solution)/shard_map/reduce_sum | solution.py:428
  25.1 0.3 select_reduce_fusion
  25.4 0.1 slice_compare_fusion
  25.5 0.1 pad_add_fusion
  25.6 0.6 fusion.6.values
  26.2 0.1 reshape_reshape.3
  26.3 0.1 copy.19
  26.4 0.1 convert_element_type.70
  26.6 0.7 copy-done.2
  27.3 30.7 %shard_map.110.sums = bf16[4,4,48,512]{3,2,1,0:T(8,128)(2,1)S(1)} custom-call(s32[640]{0:T(1024)S(1)} %add_select_fusion.table, s32[49]{0:T(128)S(1)} %convert_reduce_fusion.1.begins, s32[1]{0:T(128)} %bitcast.5.rank, bf16[4,4,48,512]{3,2,1,0:T(8,128)(2,1)S(1)} %get-tuple-element.9.tokens, f32[1,2048]{1,0:T(1,128)S(1)} %bitcast.29, s32[8,192]{1,0:T(8,128)S(1)} %bitcast.27, ...), custom_call_target="tpu_custom_call" | custom-call | tf_op jit(solution)/shard_map/pallas_call | solution.py:388
  58.0 18.2 %shard_map.111 = bf16[48,512]{1,0:T(8,128)(2,1)S(1)} custom-call(bf16[4,4,48,512]{3,2,1,0:T(8,128)(2,1)S(1)} %shard_map.110.sums), custom_call_target="tpu_custom_call" | custom-call | tf_op jit(solution)/shard_map/pallas_call | solution.py:300
  76.3 0.6 copy.32
  (24 shorter events, 0.2 us)
Async XLA Ops:
  3.8 0.8 %copy-start = (bf16[1,1,256,128]{3,2,1,0:T(8,128)(2,1)S(1)}, bf16[1,1,256,128]{3,2,1,0:T(8,128)(2,1)}, u32[]{:S(2)}) copy-start(bf16[1,1,256,128]{3,2,1,0:T(8,128)(2,1)} %param.18) | copy-start | bytes 196612
  4.7 0.8 %copy-start.1 = (bf16[48,512]{1,0:T(8,128)(2,1)S(1)}, bf16[48,512]{1,0:T(8,128)(2,1)}, u32[]{:S(2)}) copy-start(bf16[48,512]{1,0:T(8,128)(2,1)} %tokens.1) | copy-start | bytes 147460
  26.6 0.7 copy-start.2
